TPU v7x, 32 devices: a whole 2x2x4 slice. The times are simulated.
32 devices in a mesh: tile: 8 (over z, y), lev: 4 (over x, core).
Axes of the slice: x: 2, y: 2, z: 4, core: 2. Of those that a mesh axis runs over, the one named last changes fastest.
Arguments:
- state: bfloat16 [4, 64, 512, 64], P(None, 'lev', 'tile'), may hold values from -6 to 6
- state_cotangent: bfloat16 [4, 64, 512, 64], P(None, 'lev', 'tile'), may hold values from -6 to 6
- diffusion: float32 [512, 64], P('tile'), may hold values from 0.05 to 0.24
- remap_weight: float32 [64, 4], replicated, may hold values from 0.05 to 0.5
- remap_band: int32 [64], replicated, may hold values from 0 to 60, as said below
- edge_table: int32 [8, 4, 4], P('tile'), may hold values from 0 to 7, as said below
- w_in: bfloat16 [1024, 256], replicated, may hold values from -0.375 to 0.375
- w_out: bfloat16 [256, 1024], replicated, may hold values from -0.1875 to 0.1875
Outputs:
- state_out: bfloat16 [4, 64, 512, 64], P(None, 'lev', 'tile')
- grad_state: bfloat16 [4, 64, 512, 64], P(None, 'lev', 'tile')
- grad_w_in: float32 [1024, 256], replicated
- grad_w_out: float32 [256, 1024], replicated
Inputs may be any that keep to these rules, and one draw needn't show every extreme that they name: `edge_table`: entry [t, e] describes edge e of tile t (0 first row, 1 last row, 2 first column, 3 last column): [t, e, 0] is the tile across it, [t, e, 1] that tile's matching edge, [t, e, 2] is 1 where the strip runs reversed and 0 else, [t, e, 3] the quarter turns 0 to 3 of the vector components. The matching is symmetric: the partner's entry points back, with the same reversal and the opposite turns modulo 4. The four edges of a tile meet four different tiles, none of them the tile itself. remap_band[k] lies between k - 2 and k + 1, clipped to the range; remap_band[0] is 0.
All inputs are finite; a program needn't handle non-finite values.
Results may differ from a plain program's by a relative error of at most 0.0075.
Values may be sent and summed in bfloat16 or wider, within the bound.
A program may use at most 128 MiB of HBM per device.

v0:
```python
import math
import jax
import jax.numpy as jnp
from jax import lax
from jax.sharding import PartitionSpec as P


def local_strips(block):
    return jnp.stack(
        [block[:, :, 0, :], block[:, :, -1, :], block[:, :, :, 0], block[:, :, :, -1]], axis=0
    )


def orient(strip, flipped, quarter):
    strip = jnp.where(flipped == 1, strip[..., ::-1], strip)
    cosine = (quarter == 0).astype(jnp.float32) - (quarter == 2).astype(jnp.float32)
    sine_part = (quarter == 1).astype(jnp.float32) - (quarter == 3).astype(jnp.float32)
    first = strip[0].astype(jnp.float32)
    second = strip[1].astype(jnp.float32)
    turned = jnp.stack(
        [cosine * first - sine_part * second, sine_part * first + cosine * second]
    ).astype(strip.dtype)
    return jnp.concatenate([turned, strip[2:]], axis=0)


def fetch_halo(block, table):
    strips = local_strips(block)
    targets = table[:, 0]
    sources = table[:, 1]
    piece = lax.all_gather(strips[None], "tile", axis=0, tiled=True)
    ranks = jnp.arange(piece.shape[0], dtype=jnp.int32)
    edge_ids = jnp.arange(4, dtype=jnp.int32)
    which = (
        (ranks[None, :, None] == targets[:, None, None])
        & (edge_ids[None, None, :] == sources[:, None, None])
    ).astype(jnp.bfloat16)
    picked = jnp.einsum("eqk,qkflc->eflc", which, piece, preferred_element_type=jnp.float32).astype(
        jnp.bfloat16
    )
    return jnp.stack([orient(picked[edge], table[edge, 2], table[edge, 3]) for edge in range(4)])


def neighbour_sum(block, halos):
    upper = jnp.concatenate([halos[0][:, :, None, :], block[:, :, :-1, :]], axis=2)
    lower = jnp.concatenate([block[:, :, 1:, :], halos[1][:, :, None, :]], axis=2)
    before = jnp.concatenate([halos[2][:, :, :, None], block[:, :, :, :-1]], axis=3)
    after = jnp.concatenate([block[:, :, :, 1:], halos[3][:, :, :, None]], axis=3)
    return upper + lower + before + after


def remap_matrix(weight, band):
    level_ids = jnp.arange(weight.shape[0], dtype=jnp.int32)
    matrix = jnp.zeros((weight.shape[0], weight.shape[0]), weight.dtype)
    for offset in range(weight.shape[1]):
        hits = (level_ids[None, :] == (band + offset)[:, None]).astype(weight.dtype)
        matrix = matrix + weight[:, offset][:, None] * hits
    return matrix


def band_remap(columns, weight, band):
    total = jnp.zeros(columns.shape, weight.dtype)
    for offset in range(weight.shape[1]):
        picked = jnp.take(columns, band + offset, axis=1).astype(weight.dtype)
        total = total + weight[:, offset][None, :, None] * picked
    return total.astype(jnp.bfloat16)


def contract(left, right, left_dim, right_dim):
    return lax.dot_general(
        left, right, (((left_dim,), (right_dim,)), ((), ())), preferred_element_type=jnp.float32
    )


def shards(state, state_cotangent, diffusion, remap_weight, remap_band, edge_table, w_in, w_out):
    tiles = lax.axis_size("tile")
    local_levels = state.shape[1]
    side = state.shape[3]
    levels = remap_weight.shape[0]
    features = w_in.shape[1]
    table = edge_table[0]
    values = state.astype(jnp.float32)
    halo = fetch_halo(state, table).astype(jnp.float32)
    moved = (values + diffusion * (neighbour_sum(values, halo) - 4.0 * values)).astype(jnp.bfloat16)
    flat_moved = moved.reshape(4, local_levels, side * side)
    flat_cotangent = state_cotangent.reshape(4, local_levels, side * side)
    whole = lax.all_to_all(flat_moved, "lev", split_axis=2, concat_axis=1, tiled=True)
    count = whole.shape[2]
    width = min(512, count)
    blocks = count // width
    remapped = band_remap(whole, remap_weight, remap_band)
    flat = remapped.reshape(features, count)

    def forward_block(index, output):
        cols = lax.dynamic_slice_in_dim(flat, index * width, width, 1)
        pre = jnp.dot(w_in, cols, preferred_element_type=jnp.float32)
        hidden = (pre * jax.nn.sigmoid(pre)).astype(jnp.bfloat16)
        result = (
            cols.astype(jnp.float32) + jnp.dot(w_out, hidden, preferred_element_type=jnp.float32)
        ).astype(jnp.bfloat16)
        return lax.dynamic_update_slice_in_dim(output, result, index * width, 1)

    output = lax.fori_loop(0, blocks, forward_block, jnp.zeros_like(flat))
    output = output.reshape(4, levels, count)
    state_back = lax.all_to_all(output, "lev", split_axis=1, concat_axis=2, tiled=True)
    grad_whole = lax.all_to_all(flat_cotangent, "lev", split_axis=2, concat_axis=1, tiled=True)
    grad_flat = grad_whole.reshape(features, count)

    def backward_block(index, carry):
        grad_in, grad_out, dflat = carry
        cols = lax.dynamic_slice_in_dim(flat, index * width, width, 1)
        grads = lax.dynamic_slice_in_dim(grad_flat, index * width, width, 1)
        pre = jnp.dot(w_in, cols, preferred_element_type=jnp.float32)
        sigma = jax.nn.sigmoid(pre)
        hidden = (pre * sigma).astype(jnp.bfloat16)
        back = contract(w_out, grads, 0, 0)
        slope = (sigma * (1.0 + pre * (1.0 - sigma)) * back).astype(jnp.bfloat16)
        grad_out = grad_out + contract(grads, hidden, 1, 1)
        grad_in = grad_in + contract(slope, cols, 1, 1)
        dcols = grads.astype(jnp.float32) + contract(w_in, slope, 0, 0)
        return (grad_in, grad_out, lax.dynamic_update_slice_in_dim(dflat, dcols, index * width, 1))

    start = (
        jnp.zeros(w_in.shape, jnp.float32),
        jnp.zeros(w_out.shape, jnp.float32),
        jnp.zeros((features, count), jnp.float32),
    )
    grad_in, grad_out, dflat = lax.fori_loop(0, blocks, backward_block, start)
    matrix = remap_matrix(remap_weight, remap_band)
    dmoved_cols = jnp.einsum(
        "kj,fkn->fjn", matrix, dflat.reshape(4, levels, count), precision=lax.Precision.HIGHEST
    ).astype(jnp.bfloat16)
    dmoved = lax.all_to_all(dmoved_cols, "lev", split_axis=1, concat_axis=2, tiled=True)
    grad_in, grad_out = lax.psum((grad_in, grad_out), ("tile", "lev"))
    dmoved = dmoved.reshape(4, local_levels, side, side)
    flux = (diffusion * dmoved.astype(jnp.float32)).astype(jnp.bfloat16)
    flux_halo = fetch_halo(flux, table).astype(jnp.float32)
    wide_flux = flux.astype(jnp.float32)
    grad_state = (
        dmoved.astype(jnp.float32) - 4.0 * wide_flux + neighbour_sum(wide_flux, flux_halo)
    ).astype(jnp.bfloat16)
    scale = 1.0 / math.sqrt(tiles * side * side)
    state_out = state_back.reshape(4, local_levels, side, side)
    return (state_out, grad_state, grad_in * scale, grad_out * scale)


def solution(mesh):
    placed = (
        P(None, "lev", "tile", None),
        P(None, "lev", "tile", None),
        P("tile", None),
        P(),
        P(),
        P("tile", None, None),
        P(),
        P(),
    )
    return jax.shard_map(
        shards,
        mesh=mesh,
        in_specs=placed,
        out_specs=(P(None, "lev", "tile", None), P(None, "lev", "tile", None), P(), P()),
        check_vma=False,
    )
```

profile of v0, /device:TPU:0, one launch (start us, length us, event | category | flops | bytes accessed | tf_op | source)
XLA Modules:
  0.0 324.4 jit_solution(15446711326868766442)
XLA Ops:
  7.2 1.0 fusion.101
  8.2 2.1 fusion.102
  21.7 2.6 fusion.99
  24.3 2.7 fusion.100
  28.0 33.0 %all-gather = bf16[32,4,16,64]{3,2,1,0:T(8,128)(2,1)S(1)} all-gather(bf16[4,4,16,64]{3,2,1,0:T(8,128)(2,1)S(1)} %pad_maximum_fusion), channel_id=2, replica_groups=mesh['tile'=8,'lev'=4] {'tile'}, dimensions={0}, use_global_device_ids=true | all-gather | bytes 294912 | tf_op jit(solution)/shard_map/all_gather | solution.py:30
  65.6 2.0 copy.300
  67.6 5.7 %fusion.28 = bf16[4,16,64,64]{3,2,1,0:T(8,128)(2,1)} fusion(f32[4,16,63,64]{3,2,1,0:T(8,128)} %get-tuple-element.457, f32[4,16,1,64]{3,2,1,0:T(1,128)S(1)} %bitcast.284, f32[4,16,1,64]{3,2,1,0:T(1,128)S(1)} %bitcast.283, f32[4,16,63,64]{3,2,1,0:T(8,128)} %get-tuple-element.456, f32[4,16,64,63]{3,2,1,0:T(8,128)} %get-tuple-element.455, ...), kind=kLoop, calls=%fused_computation.46 | loop fusion | flops 3407872 | bytes 5259264 | tf_op jit(solution)/shard_map/convert_element_type | solution.py:83
  73.3 7.3 %copy.332 = bf16[4,16,64,64]{1,0,3,2:T(4,128)(2,1)} copy(bf16[4,16,64,64]{3,2,1,0:T(8,128)(2,1)} %fusion.28) | data formatting | bytes 1048576 | tf_op jit(solution)/shard_map/reshape | solution.py:84
  80.7 6.5 %reshape.228 = bf16[4,2,32768]{2,1,0:T(2,128)(2,1)} reshape(bf16[4096,4,16]{2,1,0:T(4,128)(2,1)} %bitcast.268) | data formatting | bytes 1048576
  87.2 3.5 %all-to-all-start = ((bf16[4,2,32768]{2,1,0:T(2,128)(2,1)}), bf16[4,2,32768]{2,1,0:T(2,128)(2,1)S(1)}, u32[]{:S(2)}, u32[]{:S(2)}) async-start(bf16[4,2,32768]{2,1,0:T(2,128)(2,1)} %reshape.228), calls=%async_computation | async-start | bytes 1048576 | tf_op jit(solution)/shard_map/all_to_all | solution.py:86
  90.7 4.9 %copy.317 = bf16[4,16,64,64]{1,0,3,2:T(4,128)(2,1)} copy(bf16[4,16,64,64]{3,2,1,0:T(8,128)(2,1)S(1)} %copy-done.10) | data formatting | bytes 1048576 | tf_op args[1]
  95.7 6.5 %reshape.230 = bf16[4,2,32768]{2,1,0:T(2,128)(2,1)} reshape(bf16[4096,4,16]{2,1,0:T(4,128)(2,1)} %bitcast.269) | data formatting | bytes 1048576
  102.1 3.7 %all-to-all-start.2 = ((bf16[4,2,32768]{2,1,0:T(2,128)(2,1)}), bf16[4,2,32768]{2,1,0:T(2,128)(2,1)S(1)}, u32[]{:S(2)}, u32[]{:S(2)}) async-start(bf16[4,2,32768]{2,1,0:T(2,128)(2,1)} %reshape.230), calls=%async_computation.2 | async-start | bytes 1048576 | tf_op jit(solution)/shard_map/all_to_all | solution.py:105
  105.9 4.1 %reshape.229 = bf16[4096,4,16]{2,1,0:T(4,128)(2,1)} reshape(bf16[4,2,32768]{2,1,0:T(2,128)(2,1)S(1)} %all-to-all-done) | data formatting | bytes 1048576
  110.0 5.5 %copy.303 = bf16[4,4,16,1024]{3,2,1,0:T(8,128)(2,1)S(1)} copy(bf16[4,4,16,1024]{2,0,3,1:T(4,128)(2,1)} %bitcast.270) | data formatting | bytes 1048576 | tf_op jit(solution)/shard_map/all_to_all | solution.py:86
  115.9 1.0 gather_fusion.2
  116.9 1.0 gather_fusion.3
  117.9 1.0 gather_fusion.1
  118.9 1.0 gather_fusion
  119.9 4.1 %reshape.231 = bf16[4096,4,16]{2,1,0:T(4,128)(2,1)} reshape(bf16[4,2,32768]{2,1,0:T(2,128)(2,1)S(1)} %all-to-all-done.2) | data formatting | bytes 1048576
  124.0 6.6 %copy.319 = bf16[4,4,16,1024]{3,2,1,0:T(8,128)(2,1)} copy(bf16[4,4,16,1024]{2,0,3,1:T(4,128)(2,1)} %bitcast.271) | data formatting | bytes 1048576 | tf_op jit(solution)/shard_map/all_to_all | solution.py:105
  130.6 0.9 add_convert_fusion
  131.5 1.1 broadcast.110.clone.1
  132.6 30.6 %while.32 = (s32[]{:T(128)}, f32[1024,256]{1,0:T(8,128)}, f32[256,1024]{1,0:T(8,128)}, f32[256,1024]{1,0:T(8,128)}, bf16[256,1024]{1,0:T(8,128)(2,1)S(1)}, /*ind...) while((s32[]{:T(128)}, f32[1024,256]{1,0:T(8,128)}, ...), condition=%wide.region_3.5_spmd.clone, body=%wide.region_2.4_spmd.clone.sunk | while | flops 1350828032 | bytes 32768392 | solution.py:127
  133.1 0.7 copy-done.9
  133.9 0.7 copy-done.5
  134.6 0.9 fusion.149
  135.5 1.1 copy.419
  136.6 2.3 fusion.150
  138.9 2.0 copy.420
  141.0 1.9 constant_dynamic-update-slice_fusion.5
  142.9 2.4 convolution_add_fusion.4
  145.3 1.8 convolution_add_fusion.5
  147.6 0.7 copy-done.9
  148.4 0.7 copy-done.5
  149.1 0.9 fusion.149
  150.0 1.1 copy.419
  151.1 2.3 fusion.150
  153.4 2.0 copy.420
  155.4 1.9 constant_dynamic-update-slice_fusion.5
  157.3 2.8 convolution_add_fusion.4
  160.1 3.1 convolution_add_fusion.5
  163.3 2.4 fusion.33
  165.6 1.2 copy.322
  166.8 3.5 %all-to-all-start.3 = ((bf16[4,64,1024]{2,0,1:T(4,128)(2,1)}), bf16[4,64,1024]{2,0,1:T(4,128)(2,1)S(1)}, u32[]{:S(2)}, u32[]{:S(2)}) async-start(bf16[4,64,1024]{2,0,1:T(4,128)(2,1)} %copy.322), calls=%async_computation.3 | async-start | bytes 1048576 | tf_op jit(solution)/shard_map/all_to_all | solution.py:132
  170.4 2.5 while.31
  170.6 0.9 fusion.137
  171.9 0.9 fusion.137
  172.9 1.2 copy.314
  174.2 5.0 %all-to-all-done.3 = bf16[4,64,1024]{2,0,1:T(4,128)(2,1)S(1)} async-done(((bf16[4,64,1024]{2,0,1:T(4,128)(2,1)}), bf16[4,64,1024]{2,0,1:T(4,128)(2,1)S(1)}, u32[]{:S(2)}, u32[]{:S(2)}) %all-to-all-start.3) | async-done | bytes 524320 | tf_op jit(solution)/shard_map/all_to_all | solution.py:132
  179.1 4.3 %all-to-all-start.1 = ((bf16[4,64,1024]{2,0,1:T(4,128)(2,1)}), bf16[4,64,1024]{2,0,1:T(4,128)(2,1)}, u32[]{:S(2)}, u32[]{:S(2)}) async-start(bf16[4,64,1024]{2,0,1:T(4,128)(2,1)} %copy.314), calls=%async_computation.1 | async-start | bytes 1048576 | tf_op jit(solution)/shard_map/all_to_all | solution.py:104
  183.9 0.8 reshape.172
  185.1 1.5 slice_reduce_fusion.1
  186.6 31.8 %all-gather.1 = bf16[32,4,16,64]{3,2,1,0:T(8,128)(2,1)S(1)} all-gather(bf16[4,4,16,64]{3,2,1,0:T(8,128)(2,1)S(1)} %pad_maximum_fusion.1), channel_id=3, replica_groups=mesh['tile'=8,'lev'=4] {'tile'}, dimensions={0}, use_global_device_ids=true | all-gather | bytes 294912 | tf_op jit(solution)/shard_map/all_gather | solution.py:30
  219.7 2.0 copy.327
  221.7 2.0 copy.328
  223.8 1.2 copy.315
  225.0 1.2 copy.316
  226.2 2.5 reshape.168
  230.0 1.0 copy-done.7
  231.6 2.7 fusion.32
  234.2 79.9 %all-reduce.3.cloned.1.call-done = (f32[1024,256]{1,0:T(8,128)}, f32[256,1024]{1,0:T(8,128)}) async-done(((f32[1024,256]{1,0:T(8,128)}, f32[256,1024]{1,0:T(8,128)}), (f32[1024,256]{1,0:T(8,128)}, f32[256,1024]{1,0:T(8,128)})) %all-reduce.3.cloned.1.call-update) | async-done | bytes 2097168 | tf_op jit(solution)/shard_map/psum | solution.py:133
  314.1 2.4 broadcast_multiply_fusion
  316.5 1.1 broadcast_multiply_fusion.1
  (145 shorter events, 9.8 us)
Async XLA Ops:
  8.2 2.1 copy-start.13
  8.2 13.5 %copy-start = (bf16[4,16,64,64]{3,2,1,0:T(8,128)(2,1)S(1)}, bf16[4,16,64,64]{3,2,1,0:T(8,128)(2,1)}, u32[]{:S(2)}) copy-start(bf16[4,16,64,64]{3,2,1,0:T(8,128)(2,1)} %param.14) | copy-start | bytes 1572868
  64.9 2.7 copy-start.12
  80.7 10.0 %copy-start.14 = (s32[64]{0:T(128)S(1)}, s32[64]{0:T(128)}, u32[]{:S(2)}) copy-start(s32[64]{0:T(128)} %param.18) | copy-start | bytes 772
  80.7 10.1 %copy-start.10 = (bf16[4,16,64,64]{3,2,1,0:T(8,128)(2,1)S(1)}, bf16[4,16,64,64]{3,2,1,0:T(8,128)(2,1)}, u32[]{:S(2)}) copy-start(bf16[4,16,64,64]{3,2,1,0:T(8,128)(2,1)} %param.15) | copy-start | bytes 1572868
  87.2 14.9 %all-to-all-start = ((bf16[4,2,32768]{2,1,0:T(2,128)(2,1)}), bf16[4,2,32768]{2,1,0:T(2,128)(2,1)S(1)}, u32[]{:S(2)}, u32[]{:S(2)}) async-start(bf16[4,2,32768]{2,1,0:T(2,128)(2,1)} %reshape.228), calls=%async_computation | async-start | bytes 1048576 | tf_op jit(solution)/shard_map/all_to_all | solution.py:86
  95.7 10.2 %copy-start.15 = (f32[64,4]{0,1:T(4,128)S(1)}, f32[64,4]{0,1:T(4,128)}, u32[]{:S(2)}) copy-start(f32[64,4]{0,1:T(4,128)} %param.17) | copy-start | bytes 3076
  102.1 17.8 %all-to-all-start.2 = ((bf16[4,2,32768]{2,1,0:T(2,128)(2,1)}), bf16[4,2,32768]{2,1,0:T(2,128)(2,1)S(1)}, u32[]{:S(2)}, u32[]{:S(2)}) async-start(bf16[4,2,32768]{2,1,0:T(2,128)(2,1)} %reshape.230), calls=%async_computation.2 | async-start | bytes 1048576 | tf_op jit(solution)/shard_map/all_to_all | solution.py:105
  130.6 2.0 copy-start.1
  132.6 1.3 copy-start.3
  132.6 1.2 copy-start.9
  132.6 2.0 copy-start.16
  133.9 0.7 copy-start.5
  140.9 4.3 %copy-start.6 = (bf16[256,512]{1,0:T(8,128)(2,1)S(1)}, bf16[256,512]{1,0:T(8,128)(2,1)}, u32[]{:S(2)}) copy-start(bf16[256,512]{1,0:T(8,128)(2,1)} %copy-done.5) | copy-start | bytes 786436 | tf_op jit(solution)/shard_map/while
  145.3 1.8 copy-start.2
  145.3 1.8 copy-start.4
  147.1 1.3 copy-start.3
  147.1 1.2 copy-start.9
  147.1 2.0 copy-start.16
  148.4 0.7 copy-start.5
  155.4 4.7 %copy-start.6 = (bf16[256,512]{1,0:T(8,128)(2,1)S(1)}, bf16[256,512]{1,0:T(8,128)(2,1)}, u32[]{:S(2)}) copy-start(bf16[256,512]{1,0:T(8,128)(2,1)} %copy-done.5) | copy-start | bytes 786436 | tf_op jit(solution)/shard_map/while
  160.1 3.1 copy-start.2
  160.1 3.1 copy-start.4
  163.3 7.2 %copy-start.17 = (bf16[256,1024]{1,0:T(8,128)(2,1)S(1)}, bf16[256,1024]{1,0:T(8,128)(2,1)}, u32[]{:S(2)}) copy-start(bf16[256,1024]{1,0:T(8,128)(2,1)} %get-tuple-element.673) | copy-start | bytes 1572868
  166.8 12.3 %all-to-all-start.3 = ((bf16[4,64,1024]{2,0,1:T(4,128)(2,1)}), bf16[4,64,1024]{2,0,1:T(4,128)(2,1)S(1)}, u32[]{:S(2)}, u32[]{:S(2)}) async-start(bf16[4,64,1024]{2,0,1:T(4,128)(2,1)} %copy.322), calls=%async_computation.3 | async-start | bytes 1048576 | tf_op jit(solution)/shard_map/all_to_all | solution.py:132
  170.3 143.8 %all-reduce.3.cloned.1.call-start = ((), (), s32[]{:S(2)}) async-start(), calls=%async_computation.4 | async-start | bytes 4194304 | tf_op jit(solution)/shard_map/psum | solution.py:133
  179.1 44.6 %all-to-all-start.1 = ((bf16[4,64,1024]{2,0,1:T(4,128)(2,1)}), bf16[4,64,1024]{2,0,1:T(4,128)(2,1)}, u32[]{:S(2)}, u32[]{:S(2)}) async-start(bf16[4,64,1024]{2,0,1:T(4,128)(2,1)} %copy.314), calls=%async_computation.1 | async-start | bytes 1048576 | tf_op jit(solution)/shard_map/all_to_all | solution.py:104
  229.4 1.6 copy-start.7
  229.4 2.2 copy-start.8
  314.1 2.4 copy-start.11
Sparse Core Ops, SparseCore 0:
  177.3 136.7 all-reduce.2
where the time goes:
time: 326 us; the launch traced here: 324 us
  local copies, waits for them, and re-layouts  95.6 us (29%)
  waiting for transfers between devices  84.8 us (26%)
  blocking collectives  64.8 us (20%)
  between operations  27.8 us (9%)
  matrix products  22.7 us (7%)
  starting transfers between devices  15 us (5%)
  other arithmetic  13.5 us (4%)
    psum x1, waiting for transfers between devices, shards(): grad_in, grad_out = lax.psum((grad_in, grad_out), ('tile', 'lev'))  79.9 us
    all_gather x2, blocking collectives, fetch_halo(): piece = lax.all_gather(strips[None], 'tile', axis=0, tiled=True)  64.8 us
    unnamed x39, local copies, waits for them, and re-layouts  28.8 us
    dot_general x8, matrix products, contract(): lax.dot_general(left, right, (((left_dim,), (right_dim,)), ((), ())), pre...  16.6 us
    dynamic_update_slice x4, local copies, waits for them, and re-layouts, backward_block(): lax.dynamic_update_slice_in_dim(dflat, dcols, index * width, 1)  7.91 us
    reshape x1, local copies, waits for them, and re-layouts, shards(): flat_moved = moved.reshape(4, local_levels, side * side)  7.34 us
    all_to_all x1, local copies, waits for them, and re-layouts, shards(): lax.all_to_all(flat_cotangent, 'lev', split_axis=2, concat_axis=1, tiled=...  6.56 us
  transfers between devices with their start and end apart: 5, of which 2 were waited for; matrix products, arithmetic and copies ran while one was open for 14% of the time, Pallas kernels for 0%

commit v1 on v0

--- a/solution.py
+++ b/solution.py
@@ -130,7 +130,7 @@
         "kj,fkn->fjn", matrix, dflat.reshape(4, levels, count), precision=lax.Precision.HIGHEST
     ).astype(jnp.bfloat16)
     dmoved = lax.all_to_all(dmoved_cols, "lev", split_axis=1, concat_axis=2, tiled=True)
-    grad_in, grad_out = lax.psum((grad_in, grad_out), ("tile", "lev"))
+    grad_in, grad_out = lax.psum(lax.psum((grad_in, grad_out), "lev"), "tile")
     dmoved = dmoved.reshape(4, local_levels, side, side)
     flux = (diffusion * dmoved.astype(jnp.float32)).astype(jnp.bfloat16)
     flux_halo = fetch_halo(flux, table).astype(jnp.float32)

time: 326 us -> 352 us (1.080)
  waiting for transfers between devices: 84.8 us -> 111 us
    psum x1 -> x2, waiting for transfers between devices: 79.9 us -> 106 us  [shards(): grad_in, grad_out = lax.psum(lax.psum((grad_in, grad_out), 'lev'), 'tile')]
  transfers between devices with their start and end apart: 5 -> 6, of which waited for: 2 -> 3; matrix products, arithmetic and copies ran while one was open for 14% -> 13% of each run, Pallas kernels for 0% -> 0%
where the time goes in v1:
time: 352 us; the launch traced here: 350 us
  waiting for transfers between devices  111 us (32%)
  local copies, waits for them, and re-layouts  95.8 us (27%)
  blocking collectives  64.5 us (18%)
  between operations  27.6 us (8%)
  matrix products  22.7 us (6%)
  starting transfers between devices  15.1 us (4%)
  other arithmetic  13.5 us (4%)
    psum x2, waiting for transfers between devices, shards(): grad_in, grad_out = lax.psum(lax.psum((grad_in, grad_out), 'lev'), 'tile')  106 us
    all_gather x2, blocking collectives, fetch_halo(): piece = lax.all_gather(strips[None], 'tile', axis=0, tiled=True)  64.5 us
    unnamed x39, local copies, waits for them, and re-layouts  28.8 us
    dot_general x8, matrix products, contract(): lax.dot_general(left, right, (((left_dim,), (right_dim,)), ((), ())), pre...  16.6 us
    dynamic_update_slice x4, local copies, waits for them, and re-layouts, backward_block(): lax.dynamic_update_slice_in_dim(dflat, dcols, index * width, 1)  7.93 us
    reshape x1, local copies, waits for them, and re-layouts, shards(): flat_moved = moved.reshape(4, local_levels, side * side)  7.36 us
  transfers between devices with their start and end apart: 6, of which 3 were waited for; matrix products, arithmetic and copies ran while one was open for 13% of the time, Pallas kernels for 0%

profile of v1, /device:TPU:0, one launch (start us, length us, event | category | flops | bytes accessed | tf_op | source)
XLA Modules:
  0.0 349.9 jit_solution(2625739264059202984)
XLA Ops:
  7.2 1.0 fusion.101
  8.2 2.1 fusion.102
  21.4 2.6 fusion.99
  24.0 2.7 fusion.100
  27.7 33.0 %all-gather = bf16[32,4,16,64]{3,2,1,0:T(8,128)(2,1)S(1)} all-gather(bf16[4,4,16,64]{3,2,1,0:T(8,128)(2,1)S(1)} %pad_maximum_fusion), channel_id=2, replica_groups=mesh['tile'=8,'lev'=4] {'tile'}, dimensions={0}, use_global_device_ids=true | all-gather | bytes 294912 | tf_op jit(solution)/shard_map/all_gather | solution.py:30
  65.5 2.0 copy.300
  67.5 5.7 %fusion.28 = bf16[4,16,64,64]{3,2,1,0:T(8,128)(2,1)} fusion(f32[4,16,63,64]{3,2,1,0:T(8,128)} %get-tuple-element.459, f32[4,16,1,64]{3,2,1,0:T(1,128)S(1)} %bitcast.284, f32[4,16,1,64]{3,2,1,0:T(1,128)S(1)} %bitcast.283, f32[4,16,63,64]{3,2,1,0:T(8,128)} %get-tuple-element.458, f32[4,16,64,63]{3,2,1,0:T(8,128)} %get-tuple-element.457, ...), kind=kLoop, calls=%fused_computation.46 | loop fusion | flops 3407872 | bytes 5259264 | tf_op jit(solution)/shard_map/convert_element_type | solution.py:83
  73.2 7.4 %copy.332 = bf16[4,16,64,64]{1,0,3,2:T(4,128)(2,1)} copy(bf16[4,16,64,64]{3,2,1,0:T(8,128)(2,1)} %fusion.28) | data formatting | bytes 1048576 | tf_op jit(solution)/shard_map/reshape | solution.py:84
  80.6 6.5 %reshape.228 = bf16[4,2,32768]{2,1,0:T(2,128)(2,1)} reshape(bf16[4096,4,16]{2,1,0:T(4,128)(2,1)} %bitcast.268) | data formatting | bytes 1048576
  87.1 3.5 all-to-all-start
  90.7 4.9 %copy.317 = bf16[4,16,64,64]{1,0,3,2:T(4,128)(2,1)} copy(bf16[4,16,64,64]{3,2,1,0:T(8,128)(2,1)S(1)} %copy-done.10) | data formatting | bytes 1048576 | tf_op args[1]
  95.6 6.5 %reshape.230 = bf16[4,2,32768]{2,1,0:T(2,128)(2,1)} reshape(bf16[4096,4,16]{2,1,0:T(4,128)(2,1)} %bitcast.269) | data formatting | bytes 1048576
  102.1 3.7 %all-to-all-start.2 = ((bf16[4,2,32768]{2,1,0:T(2,128)(2,1)}), bf16[4,2,32768]{2,1,0:T(2,128)(2,1)S(1)}, u32[]{:S(2)}, u32[]{:S(2)}) async-start(bf16[4,2,32768]{2,1,0:T(2,128)(2,1)} %reshape.230), calls=%async_computation.2 | async-start | bytes 1048576 | tf_op jit(solution)/shard_map/all_to_all | solution.py:105
  105.8 4.1 %reshape.229 = bf16[4096,4,16]{2,1,0:T(4,128)(2,1)} reshape(bf16[4,2,32768]{2,1,0:T(2,128)(2,1)S(1)} %all-to-all-done) | data formatting | bytes 1048576
  109.9 5.5 %copy.303 = bf16[4,4,16,1024]{3,2,1,0:T(8,128)(2,1)S(1)} copy(bf16[4,4,16,1024]{2,0,3,1:T(4,128)(2,1)} %bitcast.270) | data formatting | bytes 1048576 | tf_op jit(solution)/shard_map/all_to_all | solution.py:86
  115.8 1.0 gather_fusion.2
  116.8 1.0 gather_fusion.3
  117.8 1.0 gather_fusion.1
  118.8 1.0 gather_fusion
  119.8 4.1 %reshape.231 = bf16[4096,4,16]{2,1,0:T(4,128)(2,1)} reshape(bf16[4,2,32768]{2,1,0:T(2,128)(2,1)S(1)} %all-to-all-done.2) | data formatting | bytes 1048576
  124.0 6.6 %copy.319 = bf16[4,4,16,1024]{3,2,1,0:T(8,128)(2,1)} copy(bf16[4,4,16,1024]{2,0,3,1:T(4,128)(2,1)} %bitcast.271) | data formatting | bytes 1048576 | tf_op jit(solution)/shard_map/all_to_all | solution.py:105
  130.5 0.9 add_convert_fusion
  131.5 1.1 broadcast.110.clone.1
  132.6 30.7 %while.32 = (s32[]{:T(128)}, f32[1024,256]{1,0:T(8,128)}, f32[256,1024]{1,0:T(8,128)}, f32[256,1024]{1,0:T(8,128)}, bf16[256,1024]{1,0:T(8,128)(2,1)S(1)}, /*ind...) while((s32[]{:T(128)}, f32[1024,256]{1,0:T(8,128)}, ...), condition=%wide.region_3.5_spmd.clone, body=%wide.region_2.4_spmd.clone.sunk | while | flops 1350828032 | bytes 32768392 | solution.py:127
  133.1 0.7 copy-done.9
  133.8 0.7 copy-done.5
  134.5 0.9 fusion.149
  135.4 1.1 copy.419
  136.5 2.3 fusion.150
  138.8 2.1 copy.420
  140.9 1.9 constant_dynamic-update-slice_fusion.5
  142.8 2.4 convolution_add_fusion.4
  145.2 1.8 convolution_add_fusion.5
  147.6 0.7 copy-done.9
  149.0 0.9 fusion.149
  149.9 1.1 copy.419
  151.0 2.3 fusion.150
  153.3 2.1 copy.420
  155.4 1.9 constant_dynamic-update-slice_fusion.5
  157.3 2.8 convolution_add_fusion.4
  160.1 3.1 convolution_add_fusion.5
  163.2 2.4 fusion.33
  165.6 1.2 copy.322
  166.8 3.5 all-to-all-start.3
  170.4 2.5 while.31
  170.6 0.9 fusion.137
  171.8 0.9 fusion.137
  172.9 1.2 copy.314
  174.1 5.0 %all-to-all-done.3 = bf16[4,64,1024]{2,0,1:T(4,128)(2,1)S(1)} async-done(((bf16[4,64,1024]{2,0,1:T(4,128)(2,1)}), bf16[4,64,1024]{2,0,1:T(4,128)(2,1)S(1)}, u32[]{:S(2)}, u32[]{:S(2)}) %all-to-all-start.3) | async-done | bytes 524320 | tf_op jit(solution)/shard_map/all_to_all | solution.py:132
  179.1 4.2 %all-to-all-start.1 = ((bf16[4,64,1024]{2,0,1:T(4,128)(2,1)}), bf16[4,64,1024]{2,0,1:T(4,128)(2,1)}, u32[]{:S(2)}, u32[]{:S(2)}) async-start(bf16[4,64,1024]{2,0,1:T(4,128)(2,1)} %copy.314), calls=%async_computation.1 | async-start | bytes 1048576 | tf_op jit(solution)/shard_map/all_to_all | solution.py:104
  184.0 0.8 reshape.172
  185.1 1.5 slice_reduce_fusion.1
  186.6 31.5 %all-gather.1 = bf16[32,4,16,64]{3,2,1,0:T(8,128)(2,1)S(1)} all-gather(bf16[4,4,16,64]{3,2,1,0:T(8,128)(2,1)S(1)} %pad_maximum_fusion.1), channel_id=3, replica_groups=mesh['tile'=8,'lev'=4] {'tile'}, dimensions={0}, use_global_device_ids=true | all-gather | bytes 294912 | tf_op jit(solution)/shard_map/all_gather | solution.py:30
  219.3 13.8 %all-reduce.7.cloned.1.call-done = (f32[1024,256]{1,0:T(8,128)}, f32[256,1024]{1,0:T(8,128)}) async-done(((f32[1024,256]{1,0:T(8,128)}, f32[256,1024]{1,0:T(8,128)}), (f32[1024,256]{1,0:T(8,128)}, f32[256,1024]{1,0:T(8,128)})) %all-reduce.7.cloned.1.call-update) | async-done | bytes 2097168 | tf_op jit(solution)/shard_map/psum | solution.py:133
  233.2 2.0 copy.327
  235.2 2.0 copy.328
  237.3 1.2 copy.315
  238.5 1.2 copy.316
  239.7 2.5 reshape.168
  243.5 1.0 copy-done.7
  245.1 2.7 fusion.32
  247.8 91.7 %all-reduce.5.cloned.1.call-done = (f32[1024,256]{1,0:T(8,128)}, f32[256,1024]{1,0:T(8,128)}) async-done(((f32[1024,256]{1,0:T(8,128)}, f32[256,1024]{1,0:T(8,128)}), (f32[1024,256]{1,0:T(8,128)}, f32[256,1024]{1,0:T(8,128)})) %all-reduce.5.cloned.1.call-update) | async-done | bytes 2097168 | tf_op jit(solution)/shard_map/psum | solution.py:133
  339.5 2.4 broadcast_multiply_fusion
  341.9 1.1 broadcast_multiply_fusion.1
  (148 shorter events, 10.8 us)
Async XLA Ops:
  8.2 2.1 copy-start.13
  8.2 13.2 %copy-start = (bf16[4,16,64,64]{3,2,1,0:T(8,128)(2,1)S(1)}, bf16[4,16,64,64]{3,2,1,0:T(8,128)(2,1)}, u32[]{:S(2)}) copy-start(bf16[4,16,64,64]{3,2,1,0:T(8,128)(2,1)} %param.14) | copy-start | bytes 1572868
  64.8 2.7 copy-start.12
  80.6 10.0 %copy-start.14 = (s32[64]{0:T(128)S(1)}, s32[64]{0:T(128)}, u32[]{:S(2)}) copy-start(s32[64]{0:T(128)} %param.18) | copy-start | bytes 772
  80.6 10.1 %copy-start.10 = (bf16[4,16,64,64]{3,2,1,0:T(8,128)(2,1)S(1)}, bf16[4,16,64,64]{3,2,1,0:T(8,128)(2,1)}, u32[]{:S(2)}) copy-start(bf16[4,16,64,64]{3,2,1,0:T(8,128)(2,1)} %param.15) | copy-start | bytes 1572868
  87.1 14.9 %all-to-all-start = ((bf16[4,2,32768]{2,1,0:T(2,128)(2,1)}), bf16[4,2,32768]{2,1,0:T(2,128)(2,1)S(1)}, u32[]{:S(2)}, u32[]{:S(2)}) async-start(bf16[4,2,32768]{2,1,0:T(2,128)(2,1)} %reshape.228), calls=%async_computation | async-start | bytes 1048576 | tf_op jit(solution)/shard_map/all_to_all | solution.py:86
  95.6 10.2 %copy-start.15 = (f32[64,4]{0,1:T(4,128)S(1)}, f32[64,4]{0,1:T(4,128)}, u32[]{:S(2)}) copy-start(f32[64,4]{0,1:T(4,128)} %param.17) | copy-start | bytes 3076
  102.1 17.8 %all-to-all-start.2 = ((bf16[4,2,32768]{2,1,0:T(2,128)(2,1)}), bf16[4,2,32768]{2,1,0:T(2,128)(2,1)S(1)}, u32[]{:S(2)}, u32[]{:S(2)}) async-start(bf16[4,2,32768]{2,1,0:T(2,128)(2,1)} %reshape.230), calls=%async_computation.2 | async-start | bytes 1048576 | tf_op jit(solution)/shard_map/all_to_all | solution.py:105
  130.5 2.0 copy-start.1
  132.6 1.3 copy-start.3
  132.6 1.2 copy-start.9
  132.6 2.0 copy-start.16
  133.8 0.7 copy-start.5
  140.9 4.3 %copy-start.6 = (bf16[256,512]{1,0:T(8,128)(2,1)S(1)}, bf16[256,512]{1,0:T(8,128)(2,1)}, u32[]{:S(2)}) copy-start(bf16[256,512]{1,0:T(8,128)(2,1)} %copy-done.5) | copy-start | bytes 786436 | tf_op jit(solution)/shard_map/while
  145.2 1.8 copy-start.2
  145.2 1.8 copy-start.4
  147.0 1.3 copy-start.3
  147.1 1.2 copy-start.9
  147.1 2.0 copy-start.16
  148.3 0.7 copy-start.5
  155.4 4.7 %copy-start.6 = (bf16[256,512]{1,0:T(8,128)(2,1)S(1)}, bf16[256,512]{1,0:T(8,128)(2,1)}, u32[]{:S(2)}) copy-start(bf16[256,512]{1,0:T(8,128)(2,1)} %copy-done.5) | copy-start | bytes 786436 | tf_op jit(solution)/shard_map/while
  160.1 3.1 copy-start.2
  160.1 3.1 copy-start.4
  163.2 7.2 %copy-start.17 = (bf16[256,1024]{1,0:T(8,128)(2,1)S(1)}, bf16[256,1024]{1,0:T(8,128)(2,1)}, u32[]{:S(2)}) copy-start(bf16[256,1024]{1,0:T(8,128)(2,1)} %get-tuple-element.679) | copy-start | bytes 1572868
  166.8 12.3 %all-to-all-start.3 = ((bf16[4,64,1024]{2,0,1:T(4,128)(2,1)}), bf16[4,64,1024]{2,0,1:T(4,128)(2,1)S(1)}, u32[]{:S(2)}, u32[]{:S(2)}) async-start(bf16[4,64,1024]{2,0,1:T(4,128)(2,1)} %copy.322), calls=%async_computation.3 | async-start | bytes 1048576 | tf_op jit(solution)/shard_map/all_to_all | solution.py:132
  170.3 62.8 %all-reduce.7.cloned.1.call-start = ((), (), s32[]{:S(2)}) async-start(), calls=%async_computation.5 | async-start | bytes 4194304 | tf_op jit(solution)/shard_map/psum | solution.py:133
  179.1 58.2 %all-to-all-start.1 = ((bf16[4,64,1024]{2,0,1:T(4,128)(2,1)}), bf16[4,64,1024]{2,0,1:T(4,128)(2,1)}, u32[]{:S(2)}, u32[]{:S(2)}) async-start(bf16[4,64,1024]{2,0,1:T(4,128)(2,1)} %copy.314), calls=%async_computation.1 | async-start | bytes 1048576 | tf_op jit(solution)/shard_map/all_to_all | solution.py:104
  183.3 156.2 %all-reduce.5.cloned.1.call-start = ((), (), s32[]{:S(2)}) async-start(), calls=%async_computation.4 | async-start | bytes 4194304 | tf_op jit(solution)/shard_map/psum | solution.py:133
  242.8 1.6 copy-start.7
  242.9 2.3 copy-start.8
  339.5 2.4 copy-start.11
Sparse Core Ops, SparseCore 0:
  174.2 58.7 all-reduce.6
  237.2 102.2 all-reduce.4
